TPU v7x, 256 devices: a whole 4x4x8 slice. The times are simulated.
256 devices in a mesh: ka: 64 (over z, x, y_hi), band: 4 (over y_lo, core).
Axes of the slice: x: 4, y: 4 (y_hi: 2, y_lo: 2; y = y_hi * 2 + y_lo), z: 8, core: 2. Of those that a mesh axis runs over, the one named last changes fastest.
Arguments:
- occupied: bfloat16 [128, 8, 4096], P('ka'), may hold values from -6 to 6
- virtual: bfloat16 [128, 128, 4096], P('ka', 'band'), may hold values from -6 to 6
- occ_energy: float32 [128, 8], P('ka'), may hold values from -2 to -0.5
- virt_energy: float32 [128, 128], P(None, 'band'), may hold values from 0.5 to 2
- partner: int32 [2, 128], replicated, may hold values from 0 to 127, as said below
- coulomb: float32 [2, 512], replicated, may hold values from 0.5 to 2
- basis: bfloat16 [512, 4096], replicated, may hold values from -0.09375 to 0.09375
Outputs:
- occ_update: bfloat16 [128, 8, 4096], P('ka', None, 'band')
- virt_update: bfloat16 [128, 128, 4096], P('ka', 'band')
Inputs may be any that keep to these rules, and one draw needn't show every extreme that they name: Each row pairs the 128 k-points: partner[q, partner[q, k]] == k and partner[q, k] != k.
All inputs are finite; a program needn't handle non-finite values.
Results may differ from a plain program's by a relative error of at most 0.012.
Values may be sent and summed in bfloat16 or wider, within the bound.
A program may use at most 64 MiB of HBM per device.

v0:
```python
import math

import jax
import jax.numpy as jnp
from jax import lax
from jax.sharding import PartitionSpec as P

FREQUENCY = 2.5
BROADENING = 0.4


def response(energy_gaps):
    shifted = FREQUENCY - energy_gaps
    return shifted / (shifted * shifted + BROADENING * BROADENING)


def contract_grid(left, right):
    return lax.dot_general(
        left, right, (((1,), (1,)), ((), ())), preferred_element_type=jnp.float32
    )


def contract_rows(left, right):
    return lax.dot_general(
        left, right, (((0,), (0,)), ((), ())), preferred_element_type=jnp.float32
    )


def shards(occupied, virtual, occ_energy, virt_energy, partner, coulomb, basis):
    local_k, occ_count, grid_count = occupied.shape
    group_count = virtual.shape[1]
    aux_count = basis.shape[0]
    transfers = partner.shape[0]
    ka_size = lax.axis_size("ka")
    band_size = lax.axis_size("band")
    total_k = local_k * ka_size
    virt_count = group_count * band_size
    slice_width = group_count * grid_count // ka_size
    gram_scale = 1.0 / math.sqrt(total_k * occ_count * virt_count * aux_count)
    occ_scale = 1.0 / math.sqrt(transfers * virt_count)
    own_k = lax.axis_index("ka") * local_k + jnp.arange(local_k, dtype=jnp.int32)

    def regroup(slices):
        picked = jnp.stack(
            [jnp.take(slices, partner[transfer], axis=0) for transfer in range(transfers)]
        )
        return lax.all_to_all(picked, "ka", split_axis=1, concat_axis=2, tiled=True)

    routed = regroup(
        lax.all_to_all(
            virtual.reshape(local_k, ka_size, slice_width),
            "ka",
            split_axis=1,
            concat_axis=0,
            tiled=True,
        )
    )
    partner_virt = routed.reshape(transfers, local_k, group_count, grid_count)
    partner_energy = jnp.take(virt_energy, jnp.take(partner, own_k, axis=1), axis=0)
    occ_total = jnp.zeros((local_k, occ_count, grid_count), jnp.float32)
    virt_terms = []
    for transfer in range(transfers):
        pair_rows = (occupied[:, :, None, :] * partner_virt[transfer][:, None, :, :]).reshape(
            -1, grid_count
        )
        project_coeffs = contract_grid(pair_rows, basis).astype(jnp.bfloat16)
        energy_gaps = partner_energy[transfer][:, None, :] - occ_energy[:, :, None]
        weights = response(energy_gaps).reshape(-1, 1)
        weighted = (project_coeffs.astype(jnp.float32) * weights).astype(jnp.bfloat16)
        gram_block = contract_rows(weighted, project_coeffs)
        coul_rows = coulomb[transfer : transfer + 1]
        totals = lax.psum(gram_block[None], ("ka", "band"))
        screen_block = (coul_rows[:, :, None] * totals * coul_rows[:, None, :] * gram_scale).astype(
            jnp.bfloat16
        )[0]
        screened = jnp.dot(project_coeffs, screen_block, preferred_element_type=jnp.float32).astype(
            jnp.bfloat16
        )
        grid_field = jnp.dot(screened, basis, preferred_element_type=jnp.float32).astype(
            jnp.bfloat16
        )
        grid_field = grid_field.reshape(local_k, occ_count, group_count, grid_count).astype(
            jnp.float32
        )
        occ_term = jnp.sum(
            grid_field * partner_virt[transfer][:, None, :, :].astype(jnp.float32), axis=2
        )
        virt_term = jnp.sum(
            grid_field * occupied[:, :, None, :].astype(jnp.float32), axis=1
        ).astype(jnp.bfloat16)
        occ_term, virt_term = (occ_term, virt_term)
        occ_total = occ_total + occ_term
        virt_terms.append(virt_term)
    stacked = jnp.stack(virt_terms).reshape(transfers, local_k, ka_size, slice_width)
    slices = lax.all_to_all(stacked, "ka", split_axis=2, concat_axis=1, tiled=True)
    returned = jnp.take(slices[0], partner[0], axis=0).astype(jnp.float32)
    transfer = 1
    returned = returned + jnp.take(slices[transfer], partner[transfer], axis=0).astype(jnp.float32)
    home_rows = lax.all_to_all(
        returned.astype(jnp.bfloat16), "ka", split_axis=0, concat_axis=1, tiled=True
    )
    virt_update = home_rows.reshape(local_k, group_count, grid_count)
    occ_share = lax.psum_scatter(
        occ_total.astype(jnp.bfloat16), "band", scatter_dimension=2, tiled=True
    ).astype(jnp.float32)
    return ((occ_share * occ_scale).astype(jnp.bfloat16), virt_update)


def solution(mesh):
    in_specs = (
        P("ka", None, None),
        P("ka", "band", None),
        P("ka", None),
        P(None, "band"),
        P(),
        P(),
        P(),
    )
    out_specs = (P("ka", None, "band"), P("ka", "band", None))
    return jax.shard_map(shards, mesh=mesh, in_specs=in_specs, out_specs=out_specs, check_vma=False)
```

profile of v0, /device:TPU:1, one launch (start us, length us, event | category | flops | bytes accessed | tf_op | source)
XLA Modules:
  0.0 464.4 jit_solution(340204252524172719)
XLA Ops:
  7.2 1.2 reshape.231
  8.4 1.3 copy.55
  9.7 15.1 %all-to-all-start = ((bf16[2,64,2048]{2,0,1:T(2,128)(2,1)}), bf16[2,64,2048]{2,0,1:T(2,128)(2,1)S(1)}, u32[]{:S(2)}, u32[]{:S(2)}) async-start(bf16[2,64,2048]{2,0,1:T(2,128)(2,1)} %copy.55), calls=%async_computation | async-start | bytes 1048576 | tf_op jit(solution)/shard_map/all_to_all | solution.py:50
  24.8 0.8 compare_and_fusion.1
  25.6 16.2 %all-to-all-done = bf16[2,64,2048]{2,0,1:T(2,128)(2,1)S(1)} async-done(((bf16[2,64,2048]{2,0,1:T(2,128)(2,1)}), bf16[2,64,2048]{2,0,1:T(2,128)(2,1)S(1)}, u32[]{:S(2)}, u32[]{:S(2)}) %all-to-all-start) | async-done | bytes 524320 | tf_op jit(solution)/shard_map/all_to_all | solution.py:50
  41.8 0.2 reshape.296
  42.0 0.9 gather_fusion.2
  43.0 0.9 gather_fusion.3
  44.2 2.0 copy.56
  46.3 7.2 %all-to-all-start.1 = ((bf16[2,128,1,2048]{3,0,2,1:T(2,128)(2,1)}), bf16[2,128,1,2048]{3,0,2,1:T(2,128)(2,1)S(1)}, u32[]{:S(2)}, u32[]{:S(2)}) async-start(bf16[2,128,1,2048]{3,0,2,1:T(2,128)(2,1)} %copy.56), calls=%async_computation.1 | async-start | bytes 2097152 | tf_op jit(solution)/shard_map/all_to_all | solution.py:47
  53.7 0.6 gather_fusion
  54.7 0.6 gather_fusion.1
  55.6 24.8 %all-to-all-done.1 = bf16[2,128,1,2048]{3,0,2,1:T(2,128)(2,1)S(1)} async-done(((bf16[2,128,1,2048]{3,0,2,1:T(2,128)(2,1)}), bf16[2,128,1,2048]{3,0,2,1:T(2,128)(2,1)S(1)}, u32[]{:S(2)}, u32[]{:S(2)}) %all-to-all-start.1) | async-done | bytes 1048608 | tf_op jit(solution)/shard_map/all_to_all | solution.py:47
  80.4 1.7 fusion.32
  82.1 0.6 copy.57
  82.9 0.6 copy.62
  83.6 0.7 broadcast_multiply_fusion
  84.4 1.4 copy-done
  85.8 2.4 convolution_convert_fusion.3
  88.2 2.4 convolution_convert_fusion.5
  90.6 1.5 convolution_bitcast_fusion
  92.1 1.6 convolution_bitcast_fusion.1
  93.8 1.1 convert_element_type.132
  94.9 257.4 %all-reduce.3.cloned.1.call-done = (f32[1,512,512]{2,1,0:T(8,128)}, f32[1,512,512]{2,1,0:T(8,128)}) async-done(((f32[1,512,512]{2,1,0:T(8,128)}, f32[1,512,512]{2,1,0:T(8,128)}), (f32[1,512,512]{2,1,0:T(8,128)}, f32[1,512,512]{2,1,0:T(8,128)})) %all-reduce.3.cloned.1.call-update) | async-done | bytes 2097168 | tf_op jit(solution)/shard_map/psum | solution.py:72
  352.3 7.6 %fusion.2 = (f32[2,8,4096]{2,1,0:T(8,128)S(1)}, bf16[512,4096]{1,0:T(8,128)(2,1)}) fusion(f32[2,32,4096]{2,1,0:T(8,128)} %convert_element_type.132, bf16[512,4096]{1,0:T(8,128)(2,1)} %param.15, bf16[512,512]{1,0:T(8,128)(2,1)S(1)} %convolution_convert_fusion.3, f32[1,512,512]{2,1,0:T(8,128)} %get-tuple-element.6, f32[512]{0:T(512)S(1)} %bitcast.114), kind=kOutput, calls=%fused_computation.12 | convolution fusion | flops 2425552896 | bytes 11274240 | tf_op jit(solution)/shard_map/dot_general | solution.py:79
  359.9 7.5 %fusion = (f32[2,8,4096]{2,1,0:T(8,128)S(1)}, bf16[512,4096]{1,0:T(8,128)(2,1)}) fusion(f32[2,32,4096]{2,1,0:T(8,128)S(1)} %convert_element_type.123, bf16[512,4096]{1,0:T(8,128)(2,1)} %param.15, bf16[512,512]{1,0:T(8,128)(2,1)S(1)} %convolution_convert_fusion.5, f32[1,512,512]{2,1,0:T(8,128)} %get-tuple-element.5, f32[512]{0:T(512)S(1)} %bitcast.113), kind=kOutput, calls=%fused_computation.10 | convolution fusion | flops 2425552896 | bytes 11274240 | tf_op jit(solution)/shard_map/dot_general | solution.py:79
  367.4 4.6 fusion.1
  372.0 0.2 convert_element_type.138
  372.2 0.2 convert_element_type.140
  372.5 1.1 copy.63
  373.6 37.6 %all_to_all.63 = bf16[2,2,64,2048]{3,1,0,2:T(2,128)(2,1)S(1)} all-to-all(bf16[2,2,64,2048]{3,1,0,2:T(2,128)(2,1)S(1)} %copy.63), channel_id=1, replica_groups=mesh['ka'=64,'band'=4] {'ka'}, dimensions={2} | all-to-all | bytes 2097152 | tf_op jit(solution)/shard_map/all_to_all | solution.py:95
  411.1 0.7 fusion.31
  411.8 0.2 reshape.304
  412.1 0.9 gather_fusion.4
  413.0 0.2 reshape.308
  413.2 0.9 gather_fusion.5
  414.1 0.3 add_convert_fusion
  414.4 0.5 broadcast.217
  414.9 1.0 reduce.1
  415.9 1.1 reshape.317
  417.0 8.1 %all-to-all-start.3 = ((bf16[64,2,2048]{2,1,0:T(2,128)(2,1)}), bf16[64,2,2048]{2,1,0:T(2,128)(2,1)S(1)}, u32[]{:S(2)}, u32[]{:S(2)}) async-start(bf16[64,2,2048]{2,1,0:T(2,128)(2,1)} %reshape.317), calls=%async_computation.4 | async-start | bytes 1048576 | tf_op jit(solution)/shard_map/all_to_all | solution.py:99
  425.2 0.7 add_convert_fusion.1
  425.9 25.1 %reduce-scatter.2.cloned.1.call-done = bf16[2,8,1024]{2,1,0:T(8,128)(2,1)} async-done(((bf16[2,8,4096]{2,1,0:T(8,128)(2,1)}), bf16[2,8,1024]{2,1,0:T(8,128)(2,1)}) %reduce-scatter.2.cloned.1.call-update) | async-done | bytes 32784 | tf_op jit(solution)/shard_map/reduce_scatter | solution.py:103
  451.1 1.4 multiply_convert_fusion.6
  452.4 0.5 reshape.318
  453.0 3.1 reduce
  456.0 0.3 all_to_all.57
  456.6 1.0 reshape.232
  (45 shorter events, 2.1 us)
Async XLA Ops:
  9.7 32.1 %all-to-all-start = ((bf16[2,64,2048]{2,0,1:T(2,128)(2,1)}), bf16[2,64,2048]{2,0,1:T(2,128)(2,1)S(1)}, u32[]{:S(2)}, u32[]{:S(2)}) async-start(bf16[2,64,2048]{2,0,1:T(2,128)(2,1)} %copy.55), calls=%async_computation | async-start | bytes 1048576 | tf_op jit(solution)/shard_map/all_to_all | solution.py:50
  43.9 9.6 %copy-start.3 = (s32[2,128]{1,0:T(2,128)S(1)}, s32[2,128]{1,0:T(2,128)}, u32[]{:S(2)}) copy-start(s32[2,128]{1,0:T(2,128)} %param.13) | copy-start | bytes 3076
  43.9 10.5 %copy-start.2 = (f32[128,32]{0,1:T(8,128)S(1)}, f32[128,32]{0,1:T(8,128)}, u32[]{:S(2)}) copy-start(f32[128,32]{0,1:T(8,128)} %param.12) | copy-start | bytes 49156
  43.9 11.4 %copy-start.5 = (f32[2,8]{1,0:T(2,128)S(1)}, f32[2,8]{1,0:T(2,128)}, u32[]{:S(2)}) copy-start(f32[2,8]{1,0:T(2,128)} %param.11) | copy-start | bytes 196
  46.3 34.2 %all-to-all-start.1 = ((bf16[2,128,1,2048]{3,0,2,1:T(2,128)(2,1)}), bf16[2,128,1,2048]{3,0,2,1:T(2,128)(2,1)S(1)}, u32[]{:S(2)}, u32[]{:S(2)}) async-start(bf16[2,128,1,2048]{3,0,2,1:T(2,128)(2,1)} %copy.56), calls=%async_computation.1 | async-start | bytes 2097152 | tf_op jit(solution)/shard_map/all_to_all | solution.py:47
  53.5 298.8 %all-reduce.3.cloned.1.call-start = ((), (), s32[]{:S(2)}) async-start(), calls=%async_computation.6 | async-start | bytes 4194304 | tf_op jit(solution)/shard_map/psum | solution.py:72
  80.4 3.2 copy-start.1
  83.6 2.2 copy-start
  90.5 3.2 copy-start.4
  417.0 35.4 %all-to-all-start.3 = ((bf16[64,2,2048]{2,1,0:T(2,128)(2,1)}), bf16[64,2,2048]{2,1,0:T(2,128)(2,1)S(1)}, u32[]{:S(2)}, u32[]{:S(2)}) async-start(bf16[64,2,2048]{2,1,0:T(2,128)(2,1)} %reshape.317), calls=%async_computation.4 | async-start | bytes 1048576 | tf_op jit(solution)/shard_map/all_to_all | solution.py:99
  425.2 25.9 %reduce-scatter.2.cloned.1.call-start = ((), (), s32[]{:S(2)}) async-start(), calls=%async_computation.5 | async-start | bytes 163840 | tf_op jit(solution)/shard_map/reduce_scatter | solution.py:103
Sparse Core Ops, SparseCore 0:
  93.8 258.4 all-reduce.2
  428.5 22.4 reduce-scatter.1
where the time goes:
time: 465 us; the launch traced here: 464 us
  waiting for transfers between devices  324 us (70%)
  blocking collectives  37.6 us (8%)
  starting transfers between devices  30.5 us (7%)
  matrix products  22.9 us (5%)
  local copies, waits for them, and re-layouts  21.1 us (5%)
  between operations  14.4 us (3%)
  other arithmetic  14.3 us (3%)
    psum x1, waiting for transfers between devices, shards(): totals = lax.psum(gram_block[None], ('ka', 'band'))  257 us
    all_to_all x1, blocking collectives, shards(): lax.all_to_all(stacked, 'ka', split_axis=2, concat_axis=1, tiled=True)  37.6 us
    reduce_scatter x1, waiting for transfers between devices, shards(): lax.psum_scatter(occ_total.astype(jnp.bfloat16), 'band', scatter_dimensio...  25.1 us
    all_to_all x1, waiting for transfers between devices, regroup(): return lax.all_to_all(picked, 'ka', split_axis=1, concat_axis=2, tiled=True)  24.8 us
    all_to_all x1, waiting for transfers between devices, shards(): lax.all_to_all(virtual.reshape(local_k, ka_size, slice_width), 'ka', spli...  16.2 us
    all_to_all x1, starting transfers between devices, shards(): lax.all_to_all(virtual.reshape(local_k, ka_size, slice_width), 'ka', spli...  15.1 us
    dot_general x2, matrix products, shards(): jnp.dot(screened, basis, preferred_element_type=jnp.float32)  15.1 us
  transfers between devices with their start and end apart: 5, of which 4 were waited for; matrix products, arithmetic and copies ran while one was open for 1% of the time, Pallas kernels for 0%

commit v1 on v0

v1 whole, which is shorter than its diff:
```python
import math

import jax
import jax.numpy as jnp
from jax import lax
from jax.sharding import PartitionSpec as P

FREQUENCY = 2.5
BROADENING = 0.4


def response(energy_gaps):
    shifted = FREQUENCY - energy_gaps
    return shifted / (shifted * shifted + BROADENING * BROADENING)


def shards(occupied, virtual, occ_energy, virt_energy, partner, coulomb, basis):
    local_k, occ_count, grid_count = occupied.shape
    group_count = virtual.shape[1]
    aux_count = basis.shape[0]
    transfers = partner.shape[0]
    ka_size = lax.axis_size("ka")
    band_size = lax.axis_size("band")
    total_k = local_k * ka_size
    virt_count = group_count * band_size
    gram_scale = 1.0 / math.sqrt(total_k * occ_count * virt_count * aux_count)
    occ_scale = 1.0 / math.sqrt(transfers * virt_count)
    own_k = lax.axis_index("ka") * local_k + jnp.arange(local_k, dtype=jnp.int32)
    width = occ_count * grid_count // ka_size

    slices = lax.all_to_all(
        occupied.reshape(local_k, ka_size, width), "ka", split_axis=1, concat_axis=0, tiled=True
    ).reshape(total_k, width)
    picked = jnp.stack([jnp.take(slices, partner[q], axis=0) for q in range(transfers)])
    partner_occ = lax.all_to_all(picked, "ka", split_axis=1, concat_axis=2, tiled=True)
    partner_occ = partner_occ.reshape(transfers, local_k, occ_count, grid_count)
    all_energy = lax.all_gather(occ_energy, "ka", axis=0, tiled=True)
    partner_energy = jnp.take(all_energy, jnp.take(partner, own_k, axis=1), axis=0)
    own_energy = jnp.take(virt_energy, own_k, axis=0)
    weights = response(own_energy[None, :, None, :] - partner_energy[:, :, :, None])

    pairs = partner_occ[:, :, :, None, :] * virtual[None, :, None, :, :]
    pairs = pairs.reshape(transfers, -1, grid_count)
    coeffs = jnp.einsum("qmr,pr->qmp", pairs, basis, preferred_element_type=jnp.float32)
    coeffs = coeffs.astype(jnp.bfloat16)
    weighted = (coeffs.astype(jnp.float32) * weights.reshape(transfers, -1, 1)).astype(jnp.bfloat16)
    gram = jnp.einsum("qmp,qms->qps", weighted, coeffs, preferred_element_type=jnp.float32)
    gram = lax.psum(gram, ("ka", "band"))
    screen = (coulomb[:, :, None] * gram * coulomb[:, None, :] * gram_scale).astype(jnp.bfloat16)
    screened = jnp.einsum("qmp,qps->qms", coeffs, screen, preferred_element_type=jnp.float32)
    screened = screened.astype(jnp.bfloat16)
    field = jnp.einsum("qmp,pr->qmr", screened, basis, preferred_element_type=jnp.float32)
    field = field.astype(jnp.bfloat16).astype(jnp.float32)
    field = field.reshape(transfers, local_k, occ_count, group_count, grid_count)
    virt_term = jnp.sum(field * partner_occ[:, :, :, None, :].astype(jnp.float32), axis=2)
    virt_update = jnp.sum(virt_term.astype(jnp.bfloat16).astype(jnp.float32), axis=0)
    virt_update = virt_update.astype(jnp.bfloat16)
    occ_term = jnp.sum(field * virtual[None, :, None, :, :].astype(jnp.float32), axis=3)

    occ_term = lax.psum_scatter(
        occ_term.astype(jnp.bfloat16), "band", scatter_dimension=3, tiled=True
    )
    sent = lax.all_to_all(
        occ_term.reshape(transfers, local_k, ka_size, -1), "ka", split_axis=2, concat_axis=1, tiled=True
    ).reshape(transfers, total_k, -1)
    home = sum(
        jnp.take(sent[q], partner[q], axis=0).astype(jnp.float32) for q in range(transfers)
    )
    home = (home * occ_scale).astype(jnp.bfloat16)
    home = lax.all_to_all(home, "ka", split_axis=0, concat_axis=1, tiled=True)
    return home.reshape(local_k, occ_count, grid_count // band_size), virt_update


def solution(mesh):
    in_specs = (
        P("ka", None, None),
        P("ka", "band", None),
        P("ka", None),
        P(None, "band"),
        P(),
        P(),
        P(),
    )
    out_specs = (P("ka", None, "band"), P("ka", "band", None))
    return jax.shard_map(shards, mesh=mesh, in_specs=in_specs, out_specs=out_specs, check_vma=False)
```

time: 465 us -> 588 us (1.26)
  blocking collectives: 37.6 us -> 154 us
  starting transfers between devices: 30.5 us -> 39.1 us
  local copies, waits for them, and re-layouts: 21.1 us -> 14 us
  waiting for transfers between devices: 324 us -> 330 us
    all_gather x0 -> x1, blocking collectives: none -> 154 us  [shards(): all_energy = lax.all_gather(occ_energy, 'ka', axis=0, tiled=True)]
    all_to_all x1 -> x0, blocking collectives: 37.6 us -> none  [shards(): lax.all_to_all(stacked, 'ka', split_axis=2, concat_axis=1, tiled=True)]
    psum x1, waiting for transfers between devices: 257 us -> 283 us  [shards(): gram = lax.psum(gram, ('ka', 'band'))]
    all_to_all x3 -> x4, waiting for transfers between devices: 41 us -> 26.4 us  [the longest x1 11 us: shards(): lax.all_to_all(picked, 'ka', split_axis=1, concat_axis=2, tiled=True)]
    all_to_all x3 -> x4, starting transfers between devices: 30.4 us -> 38.8 us  [the longest x1 15.1 us: shards(): lax.all_to_all(occupied.reshape(local_k, ka_size, width), 'ka', split_axi...]
    dot_general x6 -> x3, matrix products: 22.9 us -> 22.3 us  [the longest x1 10.9 us: shards(): jnp.einsum('qmp,pr->qmr', screened, basis, preferred_element_type=jnp.flo...]
  transfers between devices with their start and end apart: 5 -> 6, of which waited for: 4 -> 5; matrix products, arithmetic and copies ran while one was open for 1% -> 2% of each run, Pallas kernels for 0% -> 0%
where the time goes in v1:
time: 588 us
  waiting for transfers between devices  330 us (56%)
  blocking collectives  154 us (26%)
  starting transfers between devices  39.1 us (7%)
  matrix products  22.3 us (4%)
  other arithmetic  14.4 us (2%)
  between operations  14.2 us (2%)
  local copies, waits for them, and re-layouts  14 us (2%)
    psum x1, waiting for transfers between devices, shards(): gram = lax.psum(gram, ('ka', 'band'))  283 us
    all_gather x1, blocking collectives, shards(): all_energy = lax.all_gather(occ_energy, 'ka', axis=0, tiled=True)  154 us
    reduce_scatter x1, waiting for transfers between devices, shards(): lax.psum_scatter(occ_term.astype(jnp.bfloat16), 'band', scatter_dimension...  20.7 us
    all_to_all x1, starting transfers between devices, shards(): lax.all_to_all(occupied.reshape(local_k, ka_size, width), 'ka', split_axi...  15.1 us
    all_to_all x1, starting transfers between devices, shards(): lax.all_to_all(occ_term.reshape(transfers, local_k, ka_size, -1), 'ka', s...  12.2 us
  transfers between devices with their start and end apart: 6, of which 5 were waited for; matrix products, arithmetic and copies ran while one was open for 2% of the time, Pallas kernels for 0%

profile of v1, /device:TPU:1, one launch (start us, length us, event | category | flops | bytes accessed | tf_op | source)
XLA Modules:
  0.0 587.8 jit_solution(8201055556663402900)
XLA Ops:
  7.2 1.0 reshape.157
  8.2 0.8 copy.34
  9.0 15.1 %all-to-all-start = ((bf16[2,64,512]{2,0,1:T(2,128)(2,1)}), bf16[2,64,512]{2,0,1:T(2,128)(2,1)S(1)}, u32[]{:S(2)}, u32[]{:S(2)}) async-start(bf16[2,64,512]{2,0,1:T(2,128)(2,1)} %copy.34), calls=%async_computation | async-start | bytes 262144 | tf_op jit(solution)/shard_map/all_to_all | solution.py:31
  24.1 0.8 compare_and_fusion
  24.9 0.8 copy.38
  25.7 0.6 gather_fusion.1
  26.3 0.1 copy.40
  26.4 0.1 compare_and_fusion.2
  26.5 0.1 reshape.215
  26.6 0.1 copy.39
  26.7 153.8 %all-gather = f32[64,2,8]{2,1,0:T(2,128)S(1)} all-gather(f32[1,2,8]{2,1,0:T(2,128)} %bitcast.75), channel_id=1, replica_groups=mesh['ka'=64,'band'=4] {'ka'}, dimensions={0}, use_global_device_ids=true | all-gather | bytes 4160 | tf_op jit(solution)/shard_map/all_gather | solution.py:37
  180.5 0.6 gather_fusion.2
  181.1 0.1 reshape.158
  181.1 0.8 gather_fusion.3
  182.0 0.8 gather_fusion.4
  182.8 0.1 select_bitcast_fusion
  183.0 1.0 copy.35
  183.9 5.0 all-to-all-start.1
  189.0 0.1 broadcast_select_fusion
  189.1 0.1 sub.37
  189.2 0.1 sub.38
  189.3 0.1 copy.37
  189.4 0.6 gather_fusion
  189.9 0.1 broadcast_select_fusion.1
  190.0 0.1 sub.35
  190.1 11.0 %all-to-all-done.1 = bf16[2,128,512]{2,0,1:T(2,128)(2,1)S(1)} async-done(((bf16[2,128,512]{2,0,1:T(2,128)(2,1)}), bf16[2,128,512]{2,0,1:T(2,128)(2,1)S(1)}, u32[]{:S(2)}, u32[]{:S(2)}) %all-to-all-start.1) | async-done | bytes 262176 | tf_op jit(solution)/shard_map/all_to_all | solution.py:35
  201.1 0.1 mul.84
  201.3 2.5 mul.87
  203.8 6.0 %bitcast_multiply_fusion = bf16[2,512,4096]{2,1,0:T(8,128)(2,1)} fusion(bf16[512,4096]{1,0:T(8,128)(2,1)} %bitcast.63, bf16[2,2,8,4096]{3,2,1,0:T(8,128)(2,1)S(1)} %mul.84), kind=kLoop, calls=%fused_computation.11 | loop fusion | flops 4194304 | bytes 12845056 | tf_op jit(solution)/shard_map/mul | solution.py:42
  209.8 9.1 %fusion.6 = bf16[2,512,512]{2,1,0:T(8,128)(2,1)S(1)} fusion(bf16[2,512,4096]{2,1,0:T(8,128)(2,1)} %bitcast_multiply_fusion, bf16[512,4096]{1,0:T(8,128)(2,1)} %param.17), kind=kOutput, calls=%fused_computation.19 | convolution fusion | flops 4295491584 | bytes 13631488 | tf_op jit(solution)/shard_map/qmr,pr->qmp/dot_general | solution.py:44
  218.9 2.3 fusion.5
  221.3 0.2 reduce-scatter.2.cloned.1.call-start
  221.5 0.1 convert_element_type.54
  221.6 282.8 %all-reduce.2.cloned.1.call-done = f32[2,512,512]{2,1,0:T(8,128)} async-done(((f32[2,512,512]{2,1,0:T(8,128)}), f32[2,512,512]{2,1,0:T(8,128)}) %all-reduce.2.cloned.1.call-update) | async-done | bytes 2097168 | tf_op jit(solution)/shard_map/psum | solution.py:48
  504.4 10.9 %fusion = (bf16[2,2,8,4096]{3,2,1,0:T(8,128)(2,1)}, bf16[2,512,4096]{2,1,0:T(8,128)(2,1)}) fusion(f32[2,32,4096]{2,1,0:T(8,128)S(1)} %convert_element_type.54, bf16[512,4096]{1,0:T(8,128)(2,1)} %param.17, bf16[2,512,512]{2,1,0:T(8,128)(2,1)S(1)} %fusion.6, f32[2,512,512]{2,1,0:T(8,128)} %all-reduce.2.cloned.1.call-done, f32[2,512]{1,0:T(2,128)S(1)} %copy-done.2), kind=kOutput, calls=%fused_computation.9 | convolution fusion | flops 4851105792 | bytes 17043456 | tf_op jit(solution)/shard_map/qmp,pr->qmr/dot_general | solution.py:52
  515.4 20.7 %reduce-scatter.2.cloned.1.call-done = bf16[2,2,8,1024]{3,2,1,0:T(8,128)(2,1)} async-done(((bf16[2,2,8,4096]{3,2,1,0:T(8,128)(2,1)}), bf16[2,2,8,1024]{3,2,1,0:T(8,128)(2,1)}) %reduce-scatter.2.cloned.1.call-update) | async-done | bytes 65552 | tf_op jit(solution)/shard_map/reduce_scatter | solution.py:60
  536.1 0.9 reshape.161
  536.9 0.7 copy.42
  537.6 12.2 %all-to-all-start.2 = ((bf16[2,2,64,128]{3,1,0,2:T(2,128)(2,1)}), bf16[2,2,64,128]{3,1,0,2:T(2,128)(2,1)S(1)}, u32[]{:S(2)}, u32[]{:S(2)}) async-start(bf16[2,2,64,128]{3,1,0,2:T(2,128)(2,1)} %copy.42), calls=%async_computation.3 | async-start | bytes 131072 | tf_op jit(solution)/shard_map/all_to_all | solution.py:63
  549.9 5.3 fusion.1
  555.2 5.7 all-to-all-done.2
  561.0 0.7 gather_fusion.5
  561.7 0.7 gather_fusion.6
  562.4 0.7 multiply_convert_fusion.5
  563.1 6.5 %all-to-all-start.3 = ((bf16[64,2,128]{2,1,0:T(2,128)(2,1)}), bf16[64,2,128]{2,1,0:T(2,128)(2,1)S(1)}, u32[]{:S(2)}, u32[]{:S(2)}) async-start(bf16[64,2,128]{2,1,0:T(2,128)(2,1)} %bitcast.23), calls=%async_computation.4 | async-start | bytes 65536 | tf_op jit(solution)/shard_map/all_to_all | solution.py:70
  569.6 1.0 convert_reduce_fusion
  570.6 9.7 %all-to-all-done.3 = bf16[64,2,128]{2,1,0:T(2,128)(2,1)S(1)} async-done(((bf16[64,2,128]{2,1,0:T(2,128)(2,1)}), bf16[64,2,128]{2,1,0:T(2,128)(2,1)S(1)}, u32[]{:S(2)}, u32[]{:S(2)}) %all-to-all-start.3) | async-done | bytes 32800 | tf_op jit(solution)/shard_map/all_to_all | solution.py:70
  580.3 0.6 reshape.162
  (24 shorter events, 0.3 us)
Async XLA Ops:
  7.2 182.1 %copy-start.1 = (f32[128,32]{0,1:T(8,128)S(1)}, f32[128,32]{0,1:T(8,128)}, u32[]{:S(2)}) copy-start(f32[128,32]{0,1:T(8,128)} %param.14) | copy-start | bytes 49156
  7.2 194.1 %copy-start = (bf16[2,32,4096]{2,1,0:T(8,128)(2,1)S(1)}, bf16[2,32,4096]{2,1,0:T(8,128)(2,1)}, u32[]{:S(2)}) copy-start(bf16[2,32,4096]{2,1,0:T(8,128)(2,1)} %param.12) | copy-start | bytes 1572868
  9.0 172.0 %all-to-all-start = ((bf16[2,64,512]{2,0,1:T(2,128)(2,1)}), bf16[2,64,512]{2,0,1:T(2,128)(2,1)S(1)}, u32[]{:S(2)}, u32[]{:S(2)}) async-start(bf16[2,64,512]{2,0,1:T(2,128)(2,1)} %copy.34), calls=%async_computation | async-start | bytes 262144 | tf_op jit(solution)/shard_map/all_to_all | solution.py:31
  183.9 17.2 %all-to-all-start.1 = ((bf16[2,128,512]{2,0,1:T(2,128)(2,1)}), bf16[2,128,512]{2,0,1:T(2,128)(2,1)S(1)}, u32[]{:S(2)}, u32[]{:S(2)}) async-start(bf16[2,128,512]{2,0,1:T(2,128)(2,1)} %copy.35), calls=%async_computation.1 | async-start | bytes 524288 | tf_op jit(solution)/shard_map/all_to_all | solution.py:35
  189.0 315.4 %all-reduce.2.cloned.1.call-start = ((), (), s32[]{:S(2)}) async-start(), calls=%async_computation.5 | async-start | bytes 4194304 | tf_op jit(solution)/shard_map/psum | solution.py:48
  218.9 285.5 %copy-start.2 = (f32[2,512]{1,0:T(2,128)S(1)}, f32[2,512]{1,0:T(2,128)}, u32[]{:S(2)}) copy-start(f32[2,512]{1,0:T(2,128)} %param.16) | copy-start | bytes 12292
  221.3 314.8 %reduce-scatter.2.cloned.1.call-start = ((), (), s32[]{:S(2)}) async-start(), calls=%async_computation.6 | async-start | bytes 327680 | tf_op jit(solution)/shard_map/reduce_scatter | solution.py:60
  537.6 23.3 %all-to-all-start.2 = ((bf16[2,2,64,128]{3,1,0,2:T(2,128)(2,1)}), bf16[2,2,64,128]{3,1,0,2:T(2,128)(2,1)S(1)}, u32[]{:S(2)}, u32[]{:S(2)}) async-start(bf16[2,2,64,128]{3,1,0,2:T(2,128)(2,1)} %copy.42), calls=%async_computation.3 | async-start | bytes 131072 | tf_op jit(solution)/shard_map/all_to_all | solution.py:63
  563.1 17.2 %all-to-all-start.3 = ((bf16[64,2,128]{2,1,0:T(2,128)(2,1)}), bf16[64,2,128]{2,1,0:T(2,128)(2,1)S(1)}, u32[]{:S(2)}, u32[]{:S(2)}) async-start(bf16[64,2,128]{2,1,0:T(2,128)(2,1)} %bitcast.23), calls=%async_computation.4 | async-start | bytes 65536 | tf_op jit(solution)/shard_map/all_to_all | solution.py:70
Sparse Core Ops, SparseCore 0:
  221.4 282.9 all-reduce.1
  515.5 20.5 reduce-scatter.1

commit v2 on v1

v2 whole, which is shorter than its diff:
```python
import functools
import math

import jax
import jax.numpy as jnp
from jax import lax
from jax.experimental import pallas as pl
from jax.experimental.pallas import tpu as pltpu
from jax.sharding import PartitionSpec as P

FREQUENCY = 2.5
BROADENING = 0.4
F32 = jnp.float32
BF16 = jnp.bfloat16
MESH = pl.DeviceIdType.MESH
PLANE_KA = 8


def response(energy_gaps):
    shifted = FREQUENCY - energy_gaps
    return shifted / (shifted * shifted + BROADENING * BROADENING)


def dot(left, right):
    return lax.dot_general(left, right, (((1,), (0,)), ((), ())), preferred_element_type=F32)


def dot_t(left, right):
    return lax.dot_general(left, right, (((1,), (1,)), ((), ())), preferred_element_type=F32)


def dot_rows(left, right):
    return lax.dot_general(left, right, (((0,), (0,)), ((), ())), preferred_element_type=F32)


def iota(shape, axis):
    return lax.broadcasted_iota(jnp.int32, shape, axis)


def ones_where(mask):
    return jnp.where(mask, 1.0, 0.0).astype(BF16)


def wait_bytes(ref, sem):
    pltpu.make_async_copy(ref, ref, sem).wait()


def kernel(
    ka_size, band_size, gram_scale, occ_scale,
    occ_ref, virt_hbm, occ_en_ref, virt_en_ref, partner_ref, coul_ref, basis_hbm,
    occ_out, virt_out,
    virt, virt_f, basis, en_s, a1_send, a1_recv, a2_send, a2_recv, occp, occ_f, en_f,
    pick_a, pick_c, fold_a, scale_s, coeffs, acc, weighted, tri_f,
    g1_send, g1_recv, g2_send, g2_recv, g3_recv, screen, screened, field, virt_acc, terms,
    cb_send, cb_recv, c1_send, c1_recv, c2_send, c2_recv,
    load_sem, send_sem, recv_sem,
):
    ka = lax.axis_index("ka")
    band = lax.axis_index("band")
    plane_size = PLANE_KA * band_size
    depth = ka_size // PLANE_KA
    place = lax.rem(ka, PLANE_KA) * band_size + band
    level = ka // PLANE_KA
    quarter = occ_ref.shape[2] // band_size
    chunks = quarter // 128

    load_virt = pltpu.make_async_copy(virt_hbm, virt, load_sem.at[0])
    load_basis = pltpu.make_async_copy(basis_hbm, basis, load_sem.at[1])
    load_virt.start()
    load_basis.start()

    def spread(source, target, index):
        @pl.loop(1, ka_size)
        def _(off):
            to = lax.rem(ka + off, ka_size)
            pltpu.make_async_remote_copy(
                src_ref=source.at[to],
                dst_ref=target.at[ka],
                send_sem=send_sem.at[index],
                recv_sem=recv_sem.at[index],
                device_id=(to, band),
                device_id_type=MESH,
            ).start()

        target[ka] = source[ka]

    en_s[...] = jnp.zeros_like(en_s)
    rest = occ_en_ref[...]
    for part in range(3):
        piece = rest.astype(BF16).astype(F32)
        for k in range(2):
            en_s[2 + 2 * part + k : 3 + 2 * part + k, 0:8] = piece[k : k + 1, :]
        rest = rest - piece
    tiles = []
    for c in range(chunks):
        for k in range(2):
            cols = pl.ds(pl.multiple_of(band * quarter + c * 128, 128), 128)
            tiles.append(occ_ref[k, :, cols].astype(F32))
    own = jnp.concatenate(tiles, axis=0).astype(BF16)
    row, col = iota((512, 128), 0), iota((512, 128), 1)
    s, e = row >> 3, row & 7
    split_a = ones_where((e < 2) & ((s >> 3) == (col & 7)) & ((s & 7) == (col >> 4)) & (((col >> 3) & 1) == e))
    sent = dot(split_a, own).reshape(64, 8, 128) + en_s[...][None]
    a1_send[...] = sent.astype(BF16)
    spread(a1_send, a1_recv, 0)

    part_row = 2 + 2 * lax.rem(ka, 3)
    moved_a = jnp.zeros((512, 512), F32)
    moved_c = jnp.zeros((512, 512), F32)
    to_c = ones_where((e == (col & 1)) & (s == (col >> 1)))
    for q in range(2):
        other = partner_ref[q : q + 1, :]
        base = (other >> 1) * 8 + (other & 1)
        to_data = ones_where((e == 2 * q + (col & 1)) & (s == (col >> 1)))
        to_en = ones_where((e == 4 + 2 * q + (col & 1)) & (s == (col >> 1)))
        moved_a += dot_t(to_data, ones_where(row == base))
        moved_a += dot_t(to_en, ones_where(row == base + part_row))
        moved_c += dot_t(to_c, ones_where(row == base + 2 * q))
    pick_a[...] = moved_a.astype(BF16)
    pick_c[...] = moved_c.astype(BF16)
    r2, c2 = iota((256, 512), 0), iota((256, 512), 1)
    fold_a[...] = ones_where(
        ((c2 & 7) == ((r2 >> 3) & 3)) & ((c2 >> 6) == (r2 & 7)) & (((c2 >> 3) & 7) == (r2 >> 5))
    )

    blocks = [(i, j) for i in range(4) for j in range(i, 4)]
    for q in range(2):
        rows_b, cols_b = [], []
        for i in range(4):
            line = coul_ref[q : q + 1, i * 128 : (i + 1) * 128]
            full = jnp.broadcast_to(line, (128, 128))
            cols_b.append(full)
            rows_b.append(full.T)
        for n, (i, j) in enumerate(blocks):
            scale_s[q, n * 128 : (n + 1) * 128, :] = rows_b[i] * cols_b[j] * gram_scale

    diag = iota((32, 32), 0) == iota((32, 32), 1)
    virt_cols = []
    for k in range(2):
        line = virt_en_ref[pl.ds(2 * ka + k, 1), :]
        full = jnp.where(diag, jnp.broadcast_to(line, (32, 32)), 0.0)
        virt_cols.append(jnp.broadcast_to(jnp.sum(full, axis=1, keepdims=True), (32, 128)))

    load_virt.wait()
    virt_f[...] = virt[...].astype(F32)

    wait_bytes(a1_recv.at[pl.ds(0, ka_size - 1)], recv_sem.at[0])
    got = a1_recv[...].astype(F32).reshape(512, 128).astype(BF16)
    a2_send[...] = dot(pick_a[...], got).reshape(64, 8, 128).astype(BF16)
    spread(a2_send, a2_recv, 1)
    wait_bytes(a2_recv.at[pl.ds(0, ka_size - 1)], recv_sem.at[1])
    got = a2_recv[...].astype(F32).reshape(512, 128).astype(BF16)
    folded = dot(fold_a[...], got)
    for c in range(chunks):
        occp[band, :, c * 128 : (c + 1) * 128] = folded[c * 32 : (c + 1) * 32].astype(BF16)
    en_f[...] = (
        a2_recv[0].astype(F32) + a2_recv[1].astype(F32) + a2_recv[2].astype(F32)
    )
    for off in range(1, band_size):
        to = lax.rem(band + off, band_size)
        pltpu.make_async_remote_copy(
            src_ref=occp.at[band],
            dst_ref=occp.at[band],
            send_sem=send_sem.at[2],
            recv_sem=recv_sem.at[2],
            device_id=(ka, to),
            device_id_type=MESH,
        ).start()
    load_basis.wait()
    wait_bytes(occp.at[pl.ds(0, band_size - 1)], recv_sem.at[2])
    occ_f[...] = occp[...].astype(F32)

    def project(q):
        for b in range(band_size):
            cols = slice(b * quarter, (b + 1) * quarter)
            right = basis[:, cols]
            for k in range(2):
                pieces = []
                for i in range(8):
                    n = (2 * q + k) * 8 + i
                    line = jnp.broadcast_to(occ_f[b, n : n + 1, :], (16, quarter)).astype(BF16)
                    pieces.append(virt[k, 0:16, cols] * line)
                    pieces.append(virt[k, 16:32, cols] * line)
                part = dot_t(jnp.concatenate(pieces, axis=0), right)
                rows = slice(k * 256, (k + 1) * 256)
                if b == 0:
                    acc[rows, :] = part
                else:
                    acc[rows, :] += part
        coeffs[q] = acc[...].astype(BF16)
        for k in range(2):
            for i in range(8):
                n = 4 + 2 * q + k
                energy = jnp.broadcast_to(en_f[n : n + 1, i : i + 1], (32, 128))
                weight = response(virt_cols[k] - energy)
                rows = slice(k * 256 + i * 32, k * 256 + (i + 1) * 32)
                for j in range(4):
                    cols = slice(j * 128, (j + 1) * 128)
                    weighted[rows, cols] = (coeffs[q, rows, cols].astype(F32) * weight).astype(BF16)
        n = 0
        for i in range(4):
            part = dot_rows(weighted[:, i * 128 : (i + 1) * 128], coeffs[q, :, i * 128 :])
            for j in range(4 - i):
                tri_f[n * 128 : (n + 1) * 128, :] = part[:, j * 128 : (j + 1) * 128]
                n += 1

        @pl.loop(0, plane_size)
        def _(c):
            g1_send[q, c] = tri_f[pl.ds(pl.multiple_of(c * 40, 8), 40), :].astype(BF16)

        @pl.loop(1, plane_size)
        def _(off):
            to = lax.rem(place + off, plane_size)
            pltpu.make_async_remote_copy(
                src_ref=g1_send.at[q, to],
                dst_ref=g1_recv.at[q, place],
                send_sem=send_sem.at[3 + q],
                recv_sem=recv_sem.at[3 + q],
                device_id=(level * PLANE_KA + to // band_size, lax.rem(to, band_size)),
                device_id_type=MESH,
            ).start()

        g1_recv[q, place] = g1_send[q, place]

    def exchange(q):
        wait_bytes(g1_recv.at[q, pl.ds(0, plane_size - 1)], recv_sem.at[3 + q])
        total = jnp.sum(g1_recv[q].astype(F32), axis=0).astype(BF16)
        g2_send[q] = total
        g2_recv[q, level] = total

        @pl.loop(1, depth)
        def _(off):
            to = lax.rem(level + off, depth)
            pltpu.make_async_remote_copy(
                src_ref=g2_send.at[q],
                dst_ref=g2_recv.at[q, level],
                send_sem=send_sem.at[5 + q],
                recv_sem=recv_sem.at[5 + q],
                device_id=(to * PLANE_KA + lax.rem(ka, PLANE_KA), band),
                device_id_type=MESH,
            ).start()

    def collect(q):
        wait_bytes(g2_recv.at[q, pl.ds(0, depth - 1)], recv_sem.at[5 + q])
        total = jnp.sum(g2_recv[q].astype(F32), axis=0)
        scale = scale_s[q, pl.ds(pl.multiple_of(place * 40, 8), 40), :]
        g3_recv[q, place] = (total * scale).astype(BF16)

        @pl.loop(1, plane_size)
        def _(off):
            to = lax.rem(place + off, plane_size)
            pltpu.make_async_remote_copy(
                src_ref=g3_recv.at[q, place],
                dst_ref=g3_recv.at[q, place],
                send_sem=send_sem.at[7 + q],
                recv_sem=recv_sem.at[7 + q],
                device_id=(level * PLANE_KA + to // band_size, lax.rem(to, band_size)),
                device_id_type=MESH,
            ).start()

    def respond(q):
        wait_bytes(g3_recv.at[q, pl.ds(0, plane_size - 1)], recv_sem.at[7 + q])

        @pl.loop(0, plane_size)
        def _(c):
            tri_f[pl.ds(pl.multiple_of(c * 40, 8), 40), :] = g3_recv[q, c].astype(F32)

        for n, (i, j) in enumerate(blocks):
            block = tri_f[n * 128 : (n + 1) * 128, :]
            screen[i * 128 : (i + 1) * 128, j * 128 : (j + 1) * 128] = block.astype(BF16)
            if i != j:
                screen[j * 128 : (j + 1) * 128, i * 128 : (i + 1) * 128] = block.T.astype(BF16)
        screened[...] = dot(coeffs[q], screen[...]).astype(BF16)
        width = field.shape[1]
        per = quarter // width
        for b in range(band_size):

            @pl.loop(0, per)
            def _(c):
                cols = pl.ds(pl.multiple_of(b * quarter + c * width, 128), width)
                inner = pl.ds(pl.multiple_of(c * width, 128), width)
                field[...] = dot(screened[...], basis[:, cols])
                for k in range(2):
                    near = virt_f[k, :, cols]
                    total = jnp.zeros((32, width), F32)
                    lines = []
                    for i in range(8):
                        n = (2 * q + k) * 8 + i
                        part = field[k * 256 + i * 32 : k * 256 + (i + 1) * 32, :]
                        total += part * occ_f[b, n : n + 1, inner]
                        lines.append(jnp.sum(part * near, axis=0, keepdims=True))
                    first = (2 * q + k) * 8
                    terms[b, first : first + 8, inner] = jnp.concatenate(lines, axis=0)
                    rounded = total.astype(BF16).astype(F32)
                    if q == 0:
                        virt_acc[k, :, cols] = rounded
                    else:
                        virt_out[k, :, cols] = (virt_acc[k, :, cols] + rounded).astype(BF16)

    project(0)
    project(1)
    exchange(0)
    exchange(1)
    collect(0)
    collect(1)
    respond(0)
    respond(1)

    cb_send[...] = terms[...].astype(BF16)
    for off in range(1, band_size):
        to = lax.rem(band + off, band_size)
        pltpu.make_async_remote_copy(
            src_ref=cb_send.at[to],
            dst_ref=cb_recv.at[band],
            send_sem=send_sem.at[9],
            recv_sem=recv_sem.at[9],
            device_id=(ka, to),
            device_id_type=MESH,
        ).start()
    cb_recv[band] = cb_send[band]
    r2, c2 = iota((512, 256), 0), iota((512, 256), 1)
    split_c = ones_where(
        ((r2 & 7) == ((c2 >> 3) & 3)) & ((r2 >> 6) == (c2 & 7)) & (((r2 >> 3) & 7) == (c2 >> 5))
    )
    r2, c2 = iota((128, 512), 0), iota((128, 512), 1)
    fold_c = ones_where(
        ((c2 & 7) == ((r2 >> 3) & 1)) & ((c2 >> 6) == (r2 & 7)) & (((c2 >> 3) & 7) == (r2 >> 4))
    )
    wait_bytes(cb_recv.at[pl.ds(0, band_size - 1)], recv_sem.at[9])
    total = jnp.sum(cb_recv[...].astype(F32), axis=0)
    tall = jnp.concatenate([total[:, c * 128 : (c + 1) * 128] for c in range(chunks)], axis=0)
    c1_send[...] = dot(split_c, tall.astype(BF16)).reshape(64, 8, 128).astype(BF16)
    spread(c1_send, c1_recv, 10)
    wait_bytes(c1_recv.at[pl.ds(0, ka_size - 1)], recv_sem.at[10])
    got = c1_recv[...].astype(F32).reshape(512, 128).astype(BF16)
    c2_send[...] = (dot(pick_c[...], got) * occ_scale).reshape(64, 8, 128).astype(BF16)
    spread(c2_send, c2_recv, 11)
    wait_bytes(c2_recv.at[pl.ds(0, ka_size - 1)], recv_sem.at[11])
    got = c2_recv[...].astype(F32).reshape(512, 128).astype(BF16)
    folded = dot(fold_c, got)
    for c in range(chunks):
        for k in range(2):
            first = c * 16 + k * 8
            occ_out[k, :, c * 128 : (c + 1) * 128] = folded[first : first + 8].astype(BF16)

    for index, buffer in ((0, a1_recv), (1, a2_recv), (10, c1_recv), (11, c2_recv)):
        wait_bytes(buffer.at[pl.ds(0, ka_size - 1)], send_sem.at[index])
    for index, buffer in ((2, occp), (9, cb_recv)):
        wait_bytes(buffer.at[pl.ds(0, band_size - 1)], send_sem.at[index])
    for q in range(2):
        wait_bytes(g1_recv.at[q, pl.ds(0, plane_size - 1)], send_sem.at[3 + q])
        wait_bytes(g2_recv.at[q, pl.ds(0, depth - 1)], send_sem.at[5 + q])
        wait_bytes(g3_recv.at[q, pl.ds(0, plane_size - 1)], send_sem.at[7 + q])


def shards(occupied, virtual, occ_energy, virt_energy, partner, coulomb, basis):
    local_k, occ_count, grid_count = occupied.shape
    group_count = virtual.shape[1]
    aux_count = basis.shape[0]
    transfers = partner.shape[0]
    ka_size = lax.axis_size("ka")
    band_size = lax.axis_size("band")
    total_k = local_k * ka_size
    virt_count = group_count * band_size
    quarter = grid_count // band_size
    gram_scale = 1.0 / math.sqrt(total_k * occ_count * virt_count * aux_count)
    occ_scale = 1.0 / math.sqrt(transfers * virt_count)
    plane = PLANE_KA * band_size
    depth = ka_size // PLANE_KA
    hop = pltpu.VMEM((ka_size, 8, 128), BF16)
    vmem = pl.BlockSpec(memory_space=pltpu.VMEM)
    hbm = pl.BlockSpec(memory_space=pl.ANY)
    scratch = dict(
        virt=pltpu.VMEM((2, 32, grid_count), BF16),
        virt_f=pltpu.VMEM((2, 32, grid_count), F32),
        basis=pltpu.VMEM((aux_count, grid_count), BF16),
        en_s=pltpu.VMEM((8, 128), F32),
        a1_send=hop,
        a1_recv=hop,
        a2_send=hop,
        a2_recv=hop,
        occp=pltpu.VMEM((band_size, 32, quarter), BF16),
        occ_f=pltpu.VMEM((band_size, 32, quarter), F32),
        en_f=pltpu.VMEM((8, 128), F32),
        pick_a=pltpu.VMEM((512, 512), BF16),
        pick_c=pltpu.VMEM((512, 512), BF16),
        fold_a=pltpu.VMEM((256, 512), BF16),
        scale_s=pltpu.VMEM((2, 1280, 128), F32),
        coeffs=pltpu.VMEM((2, 512, aux_count), BF16),
        acc=pltpu.VMEM((512, aux_count), F32),
        weighted=pltpu.VMEM((512, aux_count), BF16),
        tri_f=pltpu.VMEM((1280, 128), F32),
        g1_send=pltpu.VMEM((2, plane, 40, 128), BF16),
        g1_recv=pltpu.VMEM((2, plane, 40, 128), BF16),
        g2_send=pltpu.VMEM((2, 40, 128), BF16),
        g2_recv=pltpu.VMEM((2, depth, 40, 128), BF16),
        g3_recv=pltpu.VMEM((2, plane, 40, 128), BF16),
        screen=pltpu.VMEM((aux_count, aux_count), BF16),
        screened=pltpu.VMEM((512, aux_count), BF16),
        field=pltpu.VMEM((512, 256), F32),
        virt_acc=pltpu.VMEM((2, 32, grid_count), F32),
        terms=pltpu.VMEM((band_size, 32, quarter), F32),
        cb_send=pltpu.VMEM((band_size, 32, quarter), BF16),
        cb_recv=pltpu.VMEM((band_size, 32, quarter), BF16),
        c1_send=hop,
        c1_recv=hop,
        c2_send=hop,
        c2_recv=hop,
        load_sem=pltpu.SemaphoreType.DMA((2,)),
        send_sem=pltpu.SemaphoreType.DMA((12,)),
        recv_sem=pltpu.SemaphoreType.DMA((12,)),
    )
    return pl.pallas_call(
        functools.partial(kernel, ka_size, band_size, gram_scale, occ_scale),
        out_shape=(
            jax.ShapeDtypeStruct((local_k, occ_count, quarter), BF16),
            jax.ShapeDtypeStruct(virtual.shape, BF16),
        ),
        in_specs=[vmem, hbm, vmem, vmem, vmem, vmem, hbm],
        out_specs=(vmem, vmem),
        scratch_shapes=list(scratch.values()),
        compiler_params=pltpu.CompilerParams(
            has_side_effects=True, vmem_limit_bytes=48 * 1024 * 1024
        ),
    )(occupied, virtual, occ_energy, virt_energy, partner, coulomb, basis)


def solution(mesh):
    in_specs = (
        P("ka", None, None),
        P("ka", "band", None),
        P("ka", None),
        P(None, "band"),
        P(),
        P(),
        P(),
    )
    out_specs = (P("ka", None, "band"), P("ka", "band", None))
    return jax.shard_map(shards, mesh=mesh, in_specs=in_specs, out_specs=out_specs, check_vma=False)
```

time: 588 us -> 107 us (0.18)
  waiting for transfers between devices: 330 us -> 0 us
  blocking collectives: 154 us -> 0 us
  Pallas kernels: 0 us -> 97.5 us
  starting transfers between devices: 39.1 us -> 0 us
  matrix products: 22.3 us -> 0 us
  other arithmetic: 14.4 us -> 0 us
  between operations: 14.2 us -> 0.65 us
    psum x1 -> x0, waiting for transfers between devices: 283 us -> none  [shards(): gram = lax.psum(gram, ('ka', 'band'))]
    all_gather x1 -> x0, blocking collectives: 154 us -> none  [shards(): all_energy = lax.all_gather(occ_energy, 'ka', axis=0, tiled=True)]
    pallas_call x0 -> x1, Pallas kernels: none -> 97.5 us  [shards(): pl.pallas_call(functools.partial(kernel, ka_size, band_size, gram_scale,...]
    all_to_all x4 -> x0, starting transfers between devices: 38.8 us -> none  [the longest x1 15.1 us: shards(): lax.all_to_all(occupied.reshape(local_k, ka_size, width), 'ka', split_axi...]
    all_to_all x4 -> x0, waiting for transfers between devices: 26.4 us -> none  [the longest x1 11 us: shards(): lax.all_to_all(picked, 'ka', split_axis=1, concat_axis=2, tiled=True)]
    dot_general x3 -> x0, matrix products: 22.3 us -> none  [the longest x1 10.9 us: shards(): jnp.einsum('qmp,pr->qmr', screened, basis, preferred_element_type=jnp.flo...]
    reduce_scatter x1 -> x0, waiting for transfers between devices: 20.7 us -> none  [shards(): lax.psum_scatter(occ_term.astype(jnp.bfloat16), 'band', scatter_dimension...]
    unnamed x8 -> x15, local copies, waits for them, and re-layouts: 0.89 us -> 8.4 us
  transfers between devices with their start and end apart: 6 -> 0, of which waited for: 5 -> 0; matrix products, arithmetic and copies ran while one was open for 2% -> 0% of each run, Pallas kernels for 0% -> 0%
where the time goes in v2:
time: 107 us
  Pallas kernels  97.5 us (91%)
  local copies, waits for them, and re-layouts  8.4 us (8%)
    pallas_call x1, Pallas kernels, shards(): pl.pallas_call(functools.partial(kernel, ka_size, band_size, gram_scale,...  97.5 us
    unnamed x15, local copies, waits for them, and re-layouts  8.4 us

profile of v2, /device:TPU:1, one launch (start us, length us, event | category | flops | bytes accessed | tf_op | source)
XLA Modules:
  0.0 106.6 jit_solution(3903260373321696957)
XLA Ops:
  0.6 0.8 copy.9.virt_en_ref
  1.4 0.0 copy-start
  1.5 2.2 %copy-done = bf16[512,4096]{1,0:T(8,128)(2,1)S(1)} copy-done((bf16[512,4096]{1,0:T(8,128)(2,1)S(1)}, bf16[512,4096]{1,0:T(8,128)(2,1)}, u32[]{:S(2)}) %copy-start) | copy-done | bytes 4194328
  3.6 0.0 copy-start.1
  3.6 1.0 copy-done.1
  4.7 0.0 copy-start.2
  4.7 0.9 copy-done.2
  5.6 0.0 copy-start.3
  5.6 0.7 copy-done.3
  6.3 0.0 copy-start.4
  6.3 0.7 copy-done.4
  7.0 0.0 copy-start.5
  7.0 0.7 copy-done.5
  7.6 97.5 %shard_map.86 = (bf16[2,8,1024]{2,1,0:T(8,128)(2,1)S(1)}, bf16[2,32,4096]{2,1,0:T(8,128)(2,1)S(1)}) custom-call(bf16[2,8,4096]{2,1,0:T(8,128)(2,1)S(1)} %copy-done.2, bf16[2,32,4096]{2,1,0:T(8,128)(2,1)S(1)} %copy-done.1, f32[2,8]{1,0:T(2,128)S(1)} %copy-done.4, f32[128,32]{1,0:T(8,128)S(1)} %copy.9.virt_en_ref, s32[2,128]{1,0:T(2,128)S(1)} %copy-done.5, ...), custom_call_target="tpu_custom_call" | custom-call | tf_op jit(solution)/shard_map/pallas_call | solution.py:413
  105.2 0.6 copy.12
  105.8 0.8 copy.13
Async XLA Ops:
  1.4 2.2 %copy-start = (bf16[512,4096]{1,0:T(8,128)(2,1)S(1)}, bf16[512,4096]{1,0:T(8,128)(2,1)}, u32[]{:S(2)}) copy-start(bf16[512,4096]{1,0:T(8,128)(2,1)} %basis_hbm.1) | copy-start | bytes 12582916
  3.6 1.0 copy-start.1
  4.7 0.9 copy-start.2
  5.6 0.7 copy-start.3
  6.3 0.7 copy-start.4
  7.0 0.7 copy-start.5

commit v3 on v2

v3 whole, which is shorter than its diff:
```python
import functools
import math

import jax
import jax.numpy as jnp
from jax import lax
from jax.experimental import pallas as pl
from jax.experimental.pallas import tpu as pltpu
from jax.sharding import PartitionSpec as P

FREQUENCY = 2.5
BROADENING = 0.4
F32 = jnp.float32
BF16 = jnp.bfloat16
MESH = pl.DeviceIdType.MESH
PLANE_KA = 8


def response(energy_gaps):
    shifted = FREQUENCY - energy_gaps
    return shifted / (shifted * shifted + BROADENING * BROADENING)


def dot(left, right):
    return lax.dot_general(left, right, (((1,), (0,)), ((), ())), preferred_element_type=F32)


def dot_t(left, right):
    return lax.dot_general(left, right, (((1,), (1,)), ((), ())), preferred_element_type=F32)


def dot_rows(left, right):
    return lax.dot_general(left, right, (((0,), (0,)), ((), ())), preferred_element_type=F32)


def iota(shape, axis):
    return lax.broadcasted_iota(jnp.int32, shape, axis)


def ones_where(mask):
    return jnp.where(mask, 1.0, 0.0).astype(BF16)


def wait_bytes(ref, sem):
    pltpu.make_async_copy(ref, ref, sem).wait()


def kernel(
    ka_size, band_size, gram_scale, occ_scale,
    occ_hbm, virt_hbm, occ_en_hbm, virt_en_hbm, partner_hbm, coul_hbm, basis_hbm,
    occ_out, virt_out,
    occ_ref, virt, occ_en_ref, virt_en_ref, partner_ref, coul_ref, basis, virt_f, en_s, en_all,
    a1_send, a1_recv, a2_send, a2_recv, occ_b, occ_f, pick_a, pick_c, scale_s, coeffs, pairs_a, pairs_b,
    acc, weighted, tri_f, g1_send, g1_recv, g2_send, g2_recv, g3_recv, screen, screened,
    field_a, field_b, virt_acc, cb_send, cb_recv, c1_send, c1_recv, c2_send, c2_recv, table,
    load_sem, send_sem, recv_sem,
):
    ka = lax.axis_index("ka")
    band = lax.axis_index("band")
    plane_size = PLANE_KA * band_size
    depth = ka_size // PLANE_KA
    place = lax.rem(ka, PLANE_KA) * band_size + band
    level = ka // PLANE_KA
    quarter = occ_hbm.shape[2] // band_size
    chunks = quarter // 128

    barrier = pltpu.get_barrier_semaphore()

    @pl.loop(1, ka_size)
    def _(off):
        to = (lax.rem(ka + off, ka_size), band)
        pl.semaphore_signal(barrier, inc=1, device_id=to, device_id_type=MESH)

    for band_off in range(1, band_size):
        near = lax.rem(band + band_off, band_size)

        @pl.loop(0, PLANE_KA)
        def _(off):
            to = (level * PLANE_KA + lax.rem(ka + off, PLANE_KA), near)
            pl.semaphore_signal(barrier, inc=1, device_id=to, device_id_type=MESH)

    loaded = (
        (occ_hbm, occ_ref), (occ_en_hbm, occ_en_ref), (partner_hbm, partner_ref), (coul_hbm, coul_ref),
        (virt_en_hbm, virt_en_ref), (partner_hbm, table), (virt_hbm, virt), (basis_hbm, basis),
    )
    loads = [pltpu.make_async_copy(a, b, load_sem.at[n]) for n, (a, b) in enumerate(loaded)]
    for load in loads:
        load.start()
    load_occ, load_occ_en, load_partner, load_coul, load_virt_en, load_table, load_virt, load_basis = loads

    def spread(source, target, index):
        @pl.loop(1, ka_size)
        def _(off):
            to = lax.rem(ka + off, ka_size)
            pltpu.make_async_remote_copy(
                src_ref=source.at[to],
                dst_ref=target.at[ka],
                send_sem=send_sem.at[index],
                recv_sem=recv_sem.at[index],
                device_id=(to, band),
                device_id_type=MESH,
            ).start()

        target[ka] = source[ka]

    row, col = iota((128, 128), 0), iota((128, 128), 1)
    slice_of, k_of = row >> 1, row & 1
    split_a = ones_where(
        ((slice_of >> 3) == (col & 7)) & ((slice_of & 7) == (col >> 4)) & (((col >> 3) & 1) == k_of)
    )
    load_occ.wait()
    tiles = []
    for c in range(chunks):
        cols = pl.ds(pl.multiple_of(band * quarter + c * 128, 128), 128)
        tiles += [occ_ref[0, :, cols].astype(F32), occ_ref[1, :, cols].astype(F32)]
    tall = jnp.concatenate(tiles, axis=0).astype(BF16)
    a1_send[...] = dot(split_a, tall).reshape(64, 2, 128).astype(BF16)
    load_occ_en.wait()
    en_s[...] = jnp.zeros_like(en_s)
    en_s[:, 0:8] = occ_en_ref[...]
    pl.semaphore_wait(barrier, ka_size - 1 + (band_size - 1) * PLANE_KA)
    spread(a1_send, a1_recv, 0)

    @pl.loop(1, ka_size)
    def _(off):
        pltpu.make_async_remote_copy(
            src_ref=en_s,
            dst_ref=en_all.at[ka],
            send_sem=send_sem.at[2],
            recv_sem=recv_sem.at[2],
            device_id=(lax.rem(ka + off, ka_size), band),
            device_id_type=MESH,
        ).start()

    en_all[ka] = en_s[...]

    load_partner.wait()
    row, col = iota((256, 128), 0), iota((256, 128), 1)
    own_k = 2 * (row >> 2) + (row & 1)
    table_a = jnp.where(((row >> 1) & 1) == 0, partner_ref[0:1, :].astype(F32), partner_ref[1:2, :].astype(F32))
    source = jnp.sum(jnp.where(col == own_k, table_a, 0.0), axis=1, keepdims=True)
    pick_a[...] = ones_where(col == source.astype(jnp.int32))
    row, col = iota((128, 128), 0), iota((128, 128), 1)
    wide_col = iota((128, 256), 1)
    moved_c = jnp.zeros((128, 256), F32)
    for q in range(2):
        chosen = jnp.where(row == col, partner_ref[q : q + 1, :].astype(F32), 0.0)
        source = jnp.sum(chosen, axis=1, keepdims=True).astype(jnp.int32)
        moved_c += jnp.where(wide_col == (source >> 1) * 4 + 2 * q + (source & 1), 1.0, 0.0)
    pick_c[...] = moved_c.astype(BF16)
    row, col = iota((256, 256), 0), iota((256, 256), 1)
    fold_a = ones_where(
        ((col & 3) == ((row >> 3) & 3)) & ((col >> 5) == (row & 7)) & (((col >> 2) & 7) == (row >> 5))
    )

    load_coul.wait()
    blocks = [(i, j) for i in range(4) for j in range(i, 4)]
    for q in range(2):
        rows_b, cols_b = [], []
        for i in range(4):
            line = coul_ref[q : q + 1, i * 128 : (i + 1) * 128]
            full = jnp.broadcast_to(line, (128, 128))
            cols_b.append(full)
            rows_b.append(full.T)
        for n, (i, j) in enumerate(blocks):
            scale_s[q, n * 128 : (n + 1) * 128, :] = rows_b[i] * cols_b[j] * gram_scale

    load_virt_en.wait()
    virt_cols = []
    for k in range(2):
        full = jnp.where(iota((32, 128), 1) == 2 * ka + k, virt_en_ref[...], 0.0)
        virt_cols.append(jnp.broadcast_to(jnp.sum(full, axis=1, keepdims=True), (32, 128)))

    load_virt.wait()
    virt_f[...] = virt[...].astype(F32)

    wait_bytes(a1_recv.at[pl.ds(0, ka_size - 1)], recv_sem.at[0])
    got = a1_recv[...].astype(F32).reshape(128, 128).astype(BF16)
    a2_send[...] = dot(pick_a[...], got).reshape(64, 4, 128).astype(BF16)
    spread(a2_send, a2_recv, 1)
    load_basis.wait()
    load_table.wait()
    wait_bytes(en_all.at[pl.ds(0, ka_size - 1)], recv_sem.at[2])
    energies = []
    for q in range(2):
        for k in range(2):
            other = table[q, 2 * ka + k]
            energies.append(en_all[other // 2, pl.ds(lax.rem(other, 2), 1), :])
    wait_bytes(a2_recv.at[pl.ds(0, ka_size - 1)], recv_sem.at[1])
    got = a2_recv[...].astype(F32).reshape(256, 128).astype(BF16)
    folded = dot(fold_a, got)
    for q in range(2):
        for c in range(chunks):
            tile = folded[c * 32 + q * 16 : c * 32 + (q + 1) * 16]
            cols = slice(c * 128, (c + 1) * 128)
            occ_b[q, band, :, cols] = tile.astype(BF16)
            occ_f[q, band, :, cols] = tile

    for q in range(2):
        for off in range(1, band_size):
            to = lax.rem(band + band_size - off, band_size)
            pltpu.make_async_remote_copy(
                src_ref=occ_b.at[q, band],
                dst_ref=occ_b.at[q, band],
                send_sem=send_sem.at[13 + q],
                recv_sem=recv_sem.at[13 + 3 * q + off - 1],
                device_id=(ka, to),
                device_id_type=MESH,
            ).start()

    def build(q, b, pairs):
        part = lax.rem(band + b, band_size)
        if b > 0:
            wait_bytes(occ_b.at[q, part], recv_sem.at[13 + 3 * q + b - 1])
            occ_f[q, part] = occ_b[q, part].astype(F32)
        cols = pl.ds(pl.multiple_of(part * quarter, 128), quarter)
        for k in range(2):
            for i in range(8):
                n = k * 8 + i
                line = jnp.broadcast_to(occ_f[q, part, n : n + 1, :], (16, quarter)).astype(BF16)
                first = k * 256 + i * 32
                pairs[first : first + 16, :] = virt[k, 0:16, cols] * line
                pairs[first + 16 : first + 32, :] = virt[k, 16:32, cols] * line
        return cols

    def project(q):
        buffers = (pairs_a, pairs_b)
        cols = build(q, 0, buffers[0])
        for b in range(band_size):
            now = cols
            if b + 1 < band_size:
                cols = build(q, b + 1, buffers[(b + 1) % 2])
            part = dot_t(buffers[b % 2][...], basis[:, now])
            if b == 0:
                acc[...] = part
            else:
                acc[...] += part
        coeffs[q] = acc[...].astype(BF16)
        for k in range(2):
            for i in range(8):
                energy = jnp.broadcast_to(energies[2 * q + k][:, i : i + 1], (32, 128))
                weight = response(virt_cols[k] - energy)
                rows = slice(k * 256 + i * 32, k * 256 + (i + 1) * 32)
                for j in range(4):
                    cols = slice(j * 128, (j + 1) * 128)
                    weighted[rows, cols] = (coeffs[q, rows, cols].astype(F32) * weight).astype(BF16)
        n = 0
        for i in range(4):
            part = dot_rows(weighted[:, i * 128 : (i + 1) * 128], coeffs[q, :, i * 128 :])
            for j in range(4 - i):
                tri_f[n * 128 : (n + 1) * 128, :] = part[:, j * 128 : (j + 1) * 128]
                n += 1

        @pl.loop(0, plane_size)
        def _(c):
            g1_send[q, c] = tri_f[pl.ds(pl.multiple_of(c * 40, 8), 40), :].astype(BF16)

        @pl.loop(1, plane_size)
        def _(off):
            to = lax.rem(place + off, plane_size)
            pltpu.make_async_remote_copy(
                src_ref=g1_send.at[q, to],
                dst_ref=g1_recv.at[q, place],
                send_sem=send_sem.at[3 + q],
                recv_sem=recv_sem.at[3 + q],
                device_id=(level * PLANE_KA + to // band_size, lax.rem(to, band_size)),
                device_id_type=MESH,
            ).start()

        g1_recv[q, place] = g1_send[q, place]

    def exchange(q):
        wait_bytes(g1_recv.at[q, pl.ds(0, plane_size - 1)], recv_sem.at[3 + q])
        total = jnp.sum(g1_recv[q].astype(F32), axis=0).astype(BF16)
        g2_send[q] = total
        g2_recv[q, level] = total

        @pl.loop(1, depth)
        def _(off):
            to = lax.rem(level + off, depth)
            pltpu.make_async_remote_copy(
                src_ref=g2_send.at[q],
                dst_ref=g2_recv.at[q, level],
                send_sem=send_sem.at[5 + q],
                recv_sem=recv_sem.at[5 + q],
                device_id=(to * PLANE_KA + lax.rem(ka, PLANE_KA), band),
                device_id_type=MESH,
            ).start()

    def collect(q):
        wait_bytes(g2_recv.at[q, pl.ds(0, depth - 1)], recv_sem.at[5 + q])
        total = jnp.sum(g2_recv[q].astype(F32), axis=0)
        scale = scale_s[q, pl.ds(pl.multiple_of(place * 40, 8), 40), :]
        g3_recv[q, place] = (total * scale).astype(BF16)

        @pl.loop(1, plane_size)
        def _(off):
            to = lax.rem(place + off, plane_size)
            pltpu.make_async_remote_copy(
                src_ref=g3_recv.at[q, place],
                dst_ref=g3_recv.at[q, place],
                send_sem=send_sem.at[7 + q],
                recv_sem=recv_sem.at[7 + q],
                device_id=(level * PLANE_KA + to // band_size, lax.rem(to, band_size)),
                device_id_type=MESH,
            ).start()

    def prepare(q):
        wait_bytes(g3_recv.at[q, pl.ds(0, plane_size - 1)], recv_sem.at[7 + q])

        @pl.loop(0, plane_size)
        def _(c):
            tri_f[pl.ds(pl.multiple_of(c * 40, 8), 40), :] = g3_recv[q, c].astype(F32)

        for n, (i, j) in enumerate(blocks):
            block = tri_f[n * 128 : (n + 1) * 128, :]
            screen[i * 128 : (i + 1) * 128, j * 128 : (j + 1) * 128] = block.astype(BF16)
            if i != j:
                screen[j * 128 : (j + 1) * 128, i * 128 : (i + 1) * 128] = block.T.astype(BF16)
        screened[...] = dot(coeffs[q], screen[...]).astype(BF16)

    def respond(q):
        step = field_a.shape[1]
        per = quarter // step

        def locate(n):
            part = lax.rem(band + 1 + n // per, band_size)
            inner = pl.multiple_of(lax.rem(n, per) * step, 128)
            cols = pl.ds(pl.multiple_of(part * quarter + inner, 128), step)
            return part, pl.ds(inner, step), cols

        def expand(n, field):
            field[...] = dot(screened[...], basis[:, locate(n)[2]])

        def contract(n, field):
            part, inner, cols = locate(n)
            for k in range(2):
                near = virt_f[k, :, cols]
                total = jnp.zeros((32, step), F32)
                lines = []
                for i in range(8):
                    first = k * 256 + i * 32
                    piece = field[first : first + 32, :]
                    total += piece * occ_f[q, part, k * 8 + i : k * 8 + i + 1, inner]
                    lines.append(jnp.sum(piece * near, axis=0, keepdims=True))
                lines = jnp.concatenate(lines, axis=0)
                cb_send[q, part, k * 8 : (k + 1) * 8, inner] = lines.astype(BF16)
                rounded = total.astype(BF16).astype(F32)
                if q == 0:
                    virt_acc[k, :, cols] = rounded
                else:
                    virt_out[k, :, cols] = (virt_acc[k, :, cols] + rounded).astype(BF16)

        expand(0, field_a)
        for j in range(band_size):

            @pl.loop(0, per // 2)
            def _(t):
                n = j * per + 2 * t
                expand(n + 1, field_b)
                contract(n, field_a)
                expand(lax.rem(n + 2, per * band_size), field_a)
                contract(n + 1, field_b)

            to = lax.rem(band + 1 + j, band_size)
            if j < band_size - 1:
                pltpu.make_async_remote_copy(
                    src_ref=cb_send.at[q, to],
                    dst_ref=cb_recv.at[q, band],
                    send_sem=send_sem.at[9 + 3 * q],
                    recv_sem=recv_sem.at[9 + 3 * q],
                    device_id=(ka, to),
                    device_id_type=MESH,
                ).start()
            else:
                cb_recv[q, band] = cb_send[q, band]

    project(0)
    project(1)
    exchange(0)
    exchange(1)
    collect(0)
    collect(1)
    prepare(0)
    respond(0)
    prepare(1)
    respond(1)

    row, col = iota((256, 128), 0), iota((256, 128), 1)
    sent = jnp.zeros((256, 128), F32)
    for q in range(2):
        split_c = ones_where(
            ((row & 3) == 2 * q + ((col >> 3) & 1)) & ((row >> 5) == (col & 7)) & (((row >> 2) & 7) == (col >> 4))
        )
        wait_bytes(cb_recv.at[q, pl.ds(0, band_size - 1)], recv_sem.at[9 + 3 * q])
        total = jnp.sum(cb_recv[q].astype(F32), axis=0)
        tall = jnp.concatenate([total[:, c * 128 : (c + 1) * 128] for c in range(chunks)], axis=0)
        sent += dot(split_c, tall.astype(BF16))
    c1_send[...] = sent.reshape(64, 4, 128).astype(BF16)
    row, col = iota((128, 128), 0), iota((128, 128), 1)
    fold_c = ones_where(
        ((col & 1) == ((row >> 3) & 1)) & ((col >> 4) == (row & 7)) & (((col >> 1) & 7) == (row >> 4))
    )
    spread(c1_send, c1_recv, 10)
    wait_bytes(c1_recv.at[pl.ds(0, ka_size - 1)], recv_sem.at[10])
    got = c1_recv[...].astype(F32).reshape(256, 128).astype(BF16)
    c2_send[...] = (dot(pick_c[...], got) * occ_scale).reshape(64, 2, 128).astype(BF16)
    spread(c2_send, c2_recv, 11)
    wait_bytes(c2_recv.at[pl.ds(0, ka_size - 1)], recv_sem.at[11])
    got = c2_recv[...].astype(F32).reshape(128, 128).astype(BF16)
    folded = dot(fold_c, got)
    for c in range(chunks):
        for k in range(2):
            first = c * 16 + k * 8
            occ_out[k, :, c * 128 : (c + 1) * 128] = folded[first : first + 8].astype(BF16)

    for index, buffer in ((0, a1_recv), (1, a2_recv), (10, c1_recv), (11, c2_recv)):
        wait_bytes(buffer.at[pl.ds(0, ka_size - 1)], send_sem.at[index])
    wait_bytes(en_all.at[pl.ds(0, ka_size - 1)], send_sem.at[2])
    for q in range(2):
        wait_bytes(cb_recv.at[q, pl.ds(0, band_size - 1)], send_sem.at[9 + 3 * q])
        wait_bytes(occ_b.at[q, pl.ds(0, band_size - 1)], send_sem.at[13 + q])
        wait_bytes(g1_recv.at[q, pl.ds(0, plane_size - 1)], send_sem.at[3 + q])
        wait_bytes(g2_recv.at[q, pl.ds(0, depth - 1)], send_sem.at[5 + q])
        wait_bytes(g3_recv.at[q, pl.ds(0, plane_size - 1)], send_sem.at[7 + q])


def shards(occupied, virtual, occ_energy, virt_energy, partner, coulomb, basis):
    local_k, occ_count, grid_count = occupied.shape
    group_count = virtual.shape[1]
    aux_count = basis.shape[0]
    transfers = partner.shape[0]
    ka_size = lax.axis_size("ka")
    band_size = lax.axis_size("band")
    total_k = local_k * ka_size
    virt_count = group_count * band_size
    quarter = grid_count // band_size
    gram_scale = 1.0 / math.sqrt(total_k * occ_count * virt_count * aux_count)
    occ_scale = 1.0 / math.sqrt(transfers * virt_count)
    plane = PLANE_KA * band_size
    depth = ka_size // PLANE_KA
    hop_2 = pltpu.VMEM((ka_size, 2, 128), BF16)
    hop_4 = pltpu.VMEM((ka_size, 4, 128), BF16)
    virt_energy = virt_energy.T
    vmem = pl.BlockSpec(memory_space=pltpu.VMEM)
    hbm = pl.BlockSpec(memory_space=pl.ANY)
    scratch = dict(
        occ=pltpu.VMEM(occupied.shape, BF16),
        virt=pltpu.VMEM(virtual.shape, BF16),
        occ_en=pltpu.VMEM(occ_energy.shape, F32),
        virt_en=pltpu.VMEM(virt_energy.shape, F32),
        partner=pltpu.VMEM(partner.shape, jnp.int32),
        coul=pltpu.VMEM(coulomb.shape, F32),
        basis=pltpu.VMEM(basis.shape, BF16),
        virt_f=pltpu.VMEM(virtual.shape, F32),
        en_s=pltpu.VMEM((2, 128), F32),
        en_all=pltpu.VMEM((ka_size, 2, 128), F32),
        a1_send=hop_2,
        a1_recv=hop_2,
        a2_send=hop_4,
        a2_recv=hop_4,
        occ_b=pltpu.VMEM((2, band_size, 16, quarter), BF16),
        occ_f=pltpu.VMEM((2, band_size, 16, quarter), F32),
        pick_a=pltpu.VMEM((256, 128), BF16),
        pick_c=pltpu.VMEM((128, 256), BF16),
        scale_s=pltpu.VMEM((2, 1280, 128), F32),
        coeffs=pltpu.VMEM((2, 512, aux_count), BF16),
        pairs_a=pltpu.VMEM((512, quarter), BF16),
        pairs_b=pltpu.VMEM((512, quarter), BF16),
        acc=pltpu.VMEM((512, aux_count), F32),
        weighted=pltpu.VMEM((512, aux_count), BF16),
        tri_f=pltpu.VMEM((1280, 128), F32),
        g1_send=pltpu.VMEM((2, plane, 40, 128), BF16),
        g1_recv=pltpu.VMEM((2, plane, 40, 128), BF16),
        g2_send=pltpu.VMEM((2, 40, 128), BF16),
        g2_recv=pltpu.VMEM((2, depth, 40, 128), BF16),
        g3_recv=pltpu.VMEM((2, plane, 40, 128), BF16),
        screen=pltpu.VMEM((aux_count, aux_count), BF16),
        screened=pltpu.VMEM((512, aux_count), BF16),
        field_a=pltpu.VMEM((512, 256), F32),
        field_b=pltpu.VMEM((512, 256), F32),
        virt_acc=pltpu.VMEM(virtual.shape, F32),
        cb_send=pltpu.VMEM((2, band_size, 16, quarter), BF16),
        cb_recv=pltpu.VMEM((2, band_size, 16, quarter), BF16),
        c1_send=hop_4,
        c1_recv=hop_4,
        c2_send=hop_2,
        c2_recv=hop_2,
        table=pltpu.SMEM(partner.shape, jnp.int32),
        load_sem=pltpu.SemaphoreType.DMA((8,)),
        send_sem=pltpu.SemaphoreType.DMA((15,)),
        recv_sem=pltpu.SemaphoreType.DMA((19,)),
    )
    return pl.pallas_call(
        functools.partial(kernel, ka_size, band_size, gram_scale, occ_scale),
        out_shape=(
            jax.ShapeDtypeStruct((local_k, occ_count, quarter), BF16),
            jax.ShapeDtypeStruct(virtual.shape, BF16),
        ),
        in_specs=[hbm] * 7,
        out_specs=(vmem, vmem),
        scratch_shapes=list(scratch.values()),
        compiler_params=pltpu.CompilerParams(
            collective_id=0, has_side_effects=True, vmem_limit_bytes=60 * 1024 * 1024
        ),
    )(occupied, virtual, occ_energy, virt_energy, partner, coulomb, basis)


def solution(mesh):
    in_specs = (
        P("ka", None, None),
        P("ka", "band", None),
        P("ka", None),
        P(None, "band"),
        P(),
        P(),
        P(),
    )
    out_specs = (P("ka", None, "band"), P("ka", "band", None))
    return jax.shard_map(shards, mesh=mesh, in_specs=in_specs, out_specs=out_specs, check_vma=False)
```

time: 107 us -> 84.9 us (0.79)
  Pallas kernels: 97.5 us -> 80.8 us
  local copies, waits for them, and re-layouts: 8.4 us -> 3.24 us
    pallas_call x1, Pallas kernels: 97.5 us -> 80.8 us  [shards(): pl.pallas_call(functools.partial(kernel, ka_size, band_size, gram_scale,...]
    unnamed x15 -> x2, local copies, waits for them, and re-layouts: 8.4 us -> 3.24 us
where the time goes in v3:
time: 84.9 us; the launch traced here: 84.7 us
  Pallas kernels  80.8 us (95%)
  local copies, waits for them, and re-layouts  3.24 us (4%)
    pallas_call x1, Pallas kernels, shards(): pl.pallas_call(functools.partial(kernel, ka_size, band_size, gram_scale,...  80.8 us
    unnamed x2, local copies, waits for them, and re-layouts  3.24 us

profile of v3, /device:TPU:1, one launch (start us, length us, event | category | flops | bytes accessed | tf_op | source)
XLA Modules:
  0.0 84.7 jit_solution(17578166309104799452)
XLA Ops:
  0.6 80.8 %shard_map.86 = (bf16[2,8,1024]{2,1,0:T(8,128)(2,1)}, bf16[2,32,4096]{2,1,0:T(8,128)(2,1)}) custom-call(bf16[2,8,4096]{2,1,0:T(8,128)(2,1)} %occ_hbm.1, bf16[2,32,4096]{2,1,0:T(8,128)(2,1)} %virt_hbm.1, f32[2,8]{1,0:T(2,128)} %occ_en_hbm.1, f32[32,128]{1,0:T(8,128)} %bitcast.1, s32[2,128]{1,0:T(2,128)} %partner_hbm.1, f32[2,512]{1,0:T(2,128)} %coul_hbm.1, ...), custom_call_target="tpu_custom_call" | custom-call | tf_op jit(solution)/shard_map/pallas_call | solution.py:494
  81.4 1.4 %copy.11 = bf16[2,8,1024]{2,1,0:T(8,128)(2,1)} copy(bf16[2,8,1024]{2,1,0:T(8,128)(2,1)} %get-tuple-element.4) | data formatting | bytes 65536
  82.8 1.9 %copy.12 = bf16[2,32,4096]{2,1,0:T(8,128)(2,1)} copy(bf16[2,32,4096]{2,1,0:T(8,128)(2,1)} %get-tuple-element.5) | data formatting | bytes 1048576

commit v4 on v3

--- a/solution.py
+++ b/solution.py
@@ -210,9 +210,6 @@
 
     def build(q, b, pairs):
         part = lax.rem(band + b, band_size)
-        if b > 0:
-            wait_bytes(occ_b.at[q, part], recv_sem.at[13 + 3 * q + b - 1])
-            occ_f[q, part] = occ_b[q, part].astype(F32)
         cols = pl.ds(pl.multiple_of(part * quarter, 128), quarter)
         for k in range(2):
             for i in range(8):
@@ -223,19 +220,25 @@
                 pairs[first + 16 : first + 32, :] = virt[k, 16:32, cols] * line
         return cols
 
+    def begin():
+        cols = build(0, 0, pairs_a)
+        build(1, 0, pairs_b)
+        acc[0] = dot_t(pairs_a[...], basis[:, cols])
+        acc[1] = dot_t(pairs_b[...], basis[:, cols])
+
     def project(q):
+        for b in range(1, band_size):
+            part = lax.rem(band + b, band_size)
+            wait_bytes(occ_b.at[q, part], recv_sem.at[13 + 3 * q + b - 1])
+            occ_f[q, part] = occ_b[q, part].astype(F32)
         buffers = (pairs_a, pairs_b)
-        cols = build(q, 0, buffers[0])
-        for b in range(band_size):
+        cols = build(q, 1, buffers[1])
+        for b in range(1, band_size):
             now = cols
             if b + 1 < band_size:
                 cols = build(q, b + 1, buffers[(b + 1) % 2])
-            part = dot_t(buffers[b % 2][...], basis[:, now])
-            if b == 0:
-                acc[...] = part
-            else:
-                acc[...] += part
-        coeffs[q] = acc[...].astype(BF16)
+            acc[q] += dot_t(buffers[b % 2][...], basis[:, now])
+        coeffs[q] = acc[q].astype(BF16)
         for k in range(2):
             for i in range(8):
                 energy = jnp.broadcast_to(energies[2 * q + k][:, i : i + 1], (32, 128))
@@ -375,6 +378,7 @@
             else:
                 cb_recv[q, band] = cb_send[q, band]
 
+    begin()
     project(0)
     project(1)
     exchange(0)
@@ -467,7 +471,7 @@
         coeffs=pltpu.VMEM((2, 512, aux_count), BF16),
         pairs_a=pltpu.VMEM((512, quarter), BF16),
         pairs_b=pltpu.VMEM((512, quarter), BF16),
-        acc=pltpu.VMEM((512, aux_count), F32),
+        acc=pltpu.VMEM((2, 512, aux_count), F32),
         weighted=pltpu.VMEM((512, aux_count), BF16),
         tri_f=pltpu.VMEM((1280, 128), F32),
         g1_send=pltpu.VMEM((2, plane, 40, 128), BF16),
@@ -477,8 +481,8 @@
         g3_recv=pltpu.VMEM((2, plane, 40, 128), BF16),
         screen=pltpu.VMEM((aux_count, aux_count), BF16),
         screened=pltpu.VMEM((512, aux_count), BF16),
-        field_a=pltpu.VMEM((512, 256), F32),
-        field_b=pltpu.VMEM((512, 256), F32),
+        field_a=pltpu.VMEM((512, 512), F32),
+        field_b=pltpu.VMEM((512, 512), F32),
         virt_acc=pltpu.VMEM(virtual.shape, F32),
         cb_send=pltpu.VMEM((2, band_size, 16, quarter), BF16),
         cb_recv=pltpu.VMEM((2, band_size, 16, quarter), BF16),

time: 84.9 us -> 83.1 us (0.979)
  Pallas kernels: 80.8 us -> 79 us
    pallas_call x1, Pallas kernels: 80.8 us -> 79 us  [shards(): pl.pallas_call(functools.partial(kernel, ka_size, band_size, gram_scale,...]
where the time goes in v4:
time: 83.1 us; the launch traced here: 82.9 us
  Pallas kernels  79 us (95%)
  local copies, waits for them, and re-layouts  3.24 us (4%)
    pallas_call x1, Pallas kernels, shards(): pl.pallas_call(functools.partial(kernel, ka_size, band_size, gram_scale,...  79 us
    unnamed x2, local copies, waits for them, and re-layouts  3.24 us

profile of v4, /device:TPU:1, one launch (start us, length us, event | category | flops | bytes accessed | tf_op | source)
XLA Modules:
  0.0 82.9 jit_solution(9635114843174439988)
XLA Ops:
  0.6 79.0 %shard_map.86 = (bf16[2,8,1024]{2,1,0:T(8,128)(2,1)}, bf16[2,32,4096]{2,1,0:T(8,128)(2,1)}) custom-call(bf16[2,8,4096]{2,1,0:T(8,128)(2,1)} %occ_hbm.1, bf16[2,32,4096]{2,1,0:T(8,128)(2,1)} %virt_hbm.1, f32[2,8]{1,0:T(2,128)} %occ_en_hbm.1, f32[32,128]{1,0:T(8,128)} %bitcast.1, s32[2,128]{1,0:T(2,128)} %partner_hbm.1, f32[2,512]{1,0:T(2,128)} %coul_hbm.1, ...), custom_call_target="tpu_custom_call" | custom-call | tf_op jit(solution)/shard_map/pallas_call | solution.py:498
  79.7 1.4 %copy.11 = bf16[2,8,1024]{2,1,0:T(8,128)(2,1)} copy(bf16[2,8,1024]{2,1,0:T(8,128)(2,1)} %get-tuple-element.4) | data formatting | bytes 65536
  81.1 1.9 %copy.12 = bf16[2,32,4096]{2,1,0:T(8,128)(2,1)} copy(bf16[2,32,4096]{2,1,0:T(8,128)(2,1)} %get-tuple-element.5) | data formatting | bytes 1048576

commit v5 on v4

--- a/solution.py
+++ b/solution.py
@@ -48,11 +48,11 @@
 def kernel(
     ka_size, band_size, gram_scale, occ_scale,
     occ_hbm, virt_hbm, occ_en_hbm, virt_en_hbm, partner_hbm, coul_hbm, basis_hbm,
-    occ_out, virt_out,
+    occ_out, virt_hbm_out,
     occ_ref, virt, occ_en_ref, virt_en_ref, partner_ref, coul_ref, basis, virt_f, en_s, en_all,
     a1_send, a1_recv, a2_send, a2_recv, occ_b, occ_f, pick_a, pick_c, scale_s, coeffs, pairs_a, pairs_b,
     acc, weighted, tri_f, g1_send, g1_recv, g2_send, g2_recv, g3_recv, screen, screened,
-    field_a, field_b, virt_acc, cb_send, cb_recv, c1_send, c1_recv, c2_send, c2_recv, table,
+    field_a, field_b, virt_acc, virt_out, cb_send, cb_recv, c1_send, c1_recv, c2_send, c2_recv, table,
     load_sem, send_sem, recv_sem,
 ):
     ka = lax.axis_index("ka")
@@ -64,21 +64,6 @@
     quarter = occ_hbm.shape[2] // band_size
     chunks = quarter // 128
 
-    barrier = pltpu.get_barrier_semaphore()
-
-    @pl.loop(1, ka_size)
-    def _(off):
-        to = (lax.rem(ka + off, ka_size), band)
-        pl.semaphore_signal(barrier, inc=1, device_id=to, device_id_type=MESH)
-
-    for band_off in range(1, band_size):
-        near = lax.rem(band + band_off, band_size)
-
-        @pl.loop(0, PLANE_KA)
-        def _(off):
-            to = (level * PLANE_KA + lax.rem(ka + off, PLANE_KA), near)
-            pl.semaphore_signal(barrier, inc=1, device_id=to, device_id_type=MESH)
-
     loaded = (
         (occ_hbm, occ_ref), (occ_en_hbm, occ_en_ref), (partner_hbm, partner_ref), (coul_hbm, coul_ref),
         (virt_en_hbm, virt_en_ref), (partner_hbm, table), (virt_hbm, virt), (basis_hbm, basis),
@@ -86,6 +71,22 @@
     loads = [pltpu.make_async_copy(a, b, load_sem.at[n]) for n, (a, b) in enumerate(loaded)]
     for load in loads:
         load.start()
+
+    barrier = pltpu.get_barrier_semaphore()
+
+    @pl.loop(1, ka_size)
+    def _(off):
+        to = (lax.rem(ka + off, ka_size), band)
+        pl.semaphore_signal(barrier, inc=1, device_id=to, device_id_type=MESH)
+
+    for band_off in range(1, band_size):
+        near = lax.rem(band + band_off, band_size)
+
+        @pl.loop(0, PLANE_KA)
+        def _(off):
+            to = (level * PLANE_KA + lax.rem(ka + off, PLANE_KA), near)
+            pl.semaphore_signal(barrier, inc=1, device_id=to, device_id_type=MESH)
+
     load_occ, load_occ_en, load_partner, load_coul, load_virt_en, load_table, load_virt, load_basis = loads
 
     def spread(source, target, index):
@@ -390,6 +391,9 @@
     prepare(1)
     respond(1)
 
+    store_virt = pltpu.make_async_copy(virt_out, virt_hbm_out, load_sem.at[8])
+    store_virt.start()
+
     row, col = iota((256, 128), 0), iota((256, 128), 1)
     sent = jnp.zeros((256, 128), F32)
     for q in range(2):
@@ -417,6 +421,8 @@
         for k in range(2):
             first = c * 16 + k * 8
             occ_out[k, :, c * 128 : (c + 1) * 128] = folded[first : first + 8].astype(BF16)
+
+    store_virt.wait()
 
     for index, buffer in ((0, a1_recv), (1, a2_recv), (10, c1_recv), (11, c2_recv)):
         wait_bytes(buffer.at[pl.ds(0, ka_size - 1)], send_sem.at[index])
@@ -484,6 +490,7 @@
         field_a=pltpu.VMEM((512, 512), F32),
         field_b=pltpu.VMEM((512, 512), F32),
         virt_acc=pltpu.VMEM(virtual.shape, F32),
+        virt_out=pltpu.VMEM(virtual.shape, BF16),
         cb_send=pltpu.VMEM((2, band_size, 16, quarter), BF16),
         cb_recv=pltpu.VMEM((2, band_size, 16, quarter), BF16),
         c1_send=hop_4,
@@ -491,7 +498,7 @@
         c2_send=hop_2,
         c2_recv=hop_2,
         table=pltpu.SMEM(partner.shape, jnp.int32),
-        load_sem=pltpu.SemaphoreType.DMA((8,)),
+        load_sem=pltpu.SemaphoreType.DMA((9,)),
         send_sem=pltpu.SemaphoreType.DMA((15,)),
         recv_sem=pltpu.SemaphoreType.DMA((19,)),
     )
@@ -502,7 +509,7 @@
             jax.ShapeDtypeStruct(virtual.shape, BF16),
         ),
         in_specs=[hbm] * 7,
-        out_specs=(vmem, vmem),
+        out_specs=(vmem, hbm),
         scratch_shapes=list(scratch.values()),
         compiler_params=pltpu.CompilerParams(
             collective_id=0, has_side_effects=True, vmem_limit_bytes=60 * 1024 * 1024

time: 83.1 us -> 82.6 us (level)
  no operation moved by 1% of the time
where the time goes in v5:
time: 82.6 us; the launch traced here: 82.4 us
  Pallas kernels  78.5 us (95%)
  local copies, waits for them, and re-layouts  3.24 us (4%)
    pallas_call x1, Pallas kernels, shards(): pl.pallas_call(functools.partial(kernel, ka_size, band_size, gram_scale,...  78.5 us
    unnamed x2, local copies, waits for them, and re-layouts  3.24 us

profile of v5, /device:TPU:1, one launch (start us, length us, event | category | flops | bytes accessed | tf_op | source)
XLA Modules:
  0.0 82.4 jit_solution(14279449472156889011)
XLA Ops:
  0.6 78.5 %shard_map.86 = (bf16[2,8,1024]{2,1,0:T(8,128)(2,1)}, bf16[2,32,4096]{2,1,0:T(8,128)(2,1)}) custom-call(bf16[2,8,4096]{2,1,0:T(8,128)(2,1)} %occ_hbm.1, bf16[2,32,4096]{2,1,0:T(8,128)(2,1)} %virt_hbm.1, f32[2,8]{1,0:T(2,128)} %occ_en_hbm.1, f32[32,128]{1,0:T(8,128)} %bitcast.1, s32[2,128]{1,0:T(2,128)} %partner_hbm.1, f32[2,512]{1,0:T(2,128)} %coul_hbm.1, ...), custom_call_target="tpu_custom_call" | custom-call | tf_op jit(solution)/shard_map/pallas_call | solution.py:505
  79.1 1.4 %copy.11 = bf16[2,8,1024]{2,1,0:T(8,128)(2,1)} copy(bf16[2,8,1024]{2,1,0:T(8,128)(2,1)} %get-tuple-element.4) | data formatting | bytes 65536
  80.5 1.9 %copy.12 = bf16[2,32,4096]{2,1,0:T(8,128)(2,1)} copy(bf16[2,32,4096]{2,1,0:T(8,128)(2,1)} %get-tuple-element.5) | data formatting | bytes 1048576
